TPU v7x, 512 devices: a whole 4x4x16 slice. The times are simulated.
512 devices in a mesh: seq: 64 (over y, z), head: 8 (over x, core).
Axes of the slice: x: 4, y: 4, z: 16, core: 2. Of those that a mesh axis runs over, the one named last changes fastest.
Arguments:
- inputs: bfloat16 [16384, 5120], P('seq', 'head'), may hold values from -0.059814453 to 0.059814453
- log_decay: float32 [16384, 80], P('seq', 'head'), may hold values from -0.6 to 0, as said below
- b_proj: bfloat16 [16384, 128], P('seq'), may hold values from -1.796875 to 1.796875
- c_proj: bfloat16 [16384, 128], P('seq'), may hold values from -1.796875 to 1.796875
- grad_out: bfloat16 [16384, 5120], P('seq', 'head'), may hold values from -0.059814453 to 0.059814453
Outputs:
- outputs: bfloat16 [16384, 5120], P('seq', 'head')
- grad_inputs: bfloat16 [16384, 5120], P('seq', 'head')
- grad_log_decay: float32 [16384, 80], P('seq', 'head')
- grad_b: float32 [16384, 128], P('seq')
- grad_c: float32 [16384, 128], P('seq')
Inputs may be any that keep to these rules, and one draw needn't show every extreme that they name: log_decay is never positive.
All inputs are finite; a program needn't handle non-finite values.
Results may differ from a plain program's by a relative error of at most 0.01.
Values sent between devices are 32-bit elements; how exact they have to be, the bound alone decides.
A program may use at most 128 MiB of HBM per device.

v0:
```python
from functools import partial

import jax
import jax.numpy as jnp
from jax import lax
from jax.sharding import PartitionSpec as P

HEADDIM = 64
STATE = 128
BLOCK = 256


HIGHEST_PRECISION = lax.Precision.HIGHEST


def entering(part, axis, combine, identity, reverse):
    count = lax.axis_size(axis)
    place = lax.axis_index(axis)
    ahead = count - 1 - place if reverse else place
    gathered = jax.tree.map(lambda a: lax.all_gather(a, axis), part)
    state = jax.tree.map(lambda a, e: jnp.zeros_like(a) + jnp.asarray(e, a.dtype), part, identity)

    def one(lap, state):
        source = count - 1 - lap if reverse else lap
        return combine(
            state, jax.tree.map(lambda a: lax.dynamic_index_in_dim(a, source, 0, False), gathered)
        )

    return lax.fori_loop(0, ahead, one, state)


def block_terms(head_signal, head_decay, b_blocks, scores):
    window = head_decay.shape[1]
    causal = jnp.tril(jnp.ones((window, window), dtype=bool))
    prefix = jnp.cumsum(head_decay, axis=1)
    spread = prefix[:, :, None] - prefix[:, None, :]
    decay_mat = jnp.where(causal, jnp.exp(jnp.where(causal, spread, 0.0)), 0.0)
    weighted = (scores * decay_mat).astype(jnp.bfloat16)
    within = jnp.einsum(
        "kts,ksp->ktp",
        weighted,
        head_signal.astype(jnp.bfloat16),
        preferred_element_type=jnp.float32,
    )
    weights = jnp.exp(prefix[:, -1:] - prefix)
    scaled = (head_signal * weights[:, :, None]).astype(jnp.bfloat16)
    states = jnp.einsum(
        "ksp,ksn->kpn", scaled, b_blocks.astype(jnp.bfloat16), preferred_element_type=jnp.float32
    )
    return (prefix, within, states, prefix[:, -1])


def head_terms(pieces, b_blocks, c_blocks, scores):
    head_signal, head_decay = pieces
    prefix, within, states, totals = block_terms(head_signal, head_decay, b_blocks, scores)
    running = jnp.zeros(states.shape[1:], jnp.float32)
    starts = [running]
    running = jnp.exp(totals[0]) * running + states[0]
    carried = jnp.einsum("ktn,kpn->ktp", c_blocks, jnp.stack(starts), precision=HIGHEST_PRECISION)
    local_out = within + jnp.exp(prefix)[:, :, None] * carried
    return (local_out, running, jnp.exp(jnp.sum(totals)))


def score_blocks(b_proj, c_proj):
    blocks = b_proj.shape[0] // BLOCK
    b_half = b_proj.reshape(blocks, BLOCK, STATE)
    c_half = c_proj.reshape(blocks, BLOCK, STATE)
    return jnp.einsum("ktn,ksn->kts", c_half, b_half, preferred_element_type=jnp.float32)


def score_grads(grad_scores, b_proj, c_proj):
    blocks = b_proj.shape[0] // BLOCK
    b_blocks = b_proj.reshape(blocks, BLOCK, STATE)
    c_blocks = c_proj.reshape(blocks, BLOCK, STATE)
    half_scores = grad_scores.astype(jnp.bfloat16)
    grad_c_part = jnp.einsum(
        "kts,ksn->ktn", half_scores, b_blocks, preferred_element_type=jnp.float32
    ).reshape(-1, STATE)
    grad_b_part = jnp.einsum(
        "kts,ktn->ksn", half_scores, c_blocks, preferred_element_type=jnp.float32
    ).reshape(-1, STATE)
    return (grad_b_part, grad_c_part)


def device_terms(signal, decays, b_rows, c_rows, scores):
    tokens, head_count = decays.shape
    blocks = tokens // BLOCK
    head_signal = signal.reshape(blocks, BLOCK, head_count, HEADDIM).transpose(2, 0, 1, 3)
    head_decay = decays.reshape(blocks, BLOCK, head_count).transpose(2, 0, 1)
    b_blocks = b_rows.reshape(blocks, BLOCK, STATE)
    c_blocks = c_rows.reshape(blocks, BLOCK, STATE)
    per_head = jax.checkpoint(
        partial(head_terms, b_blocks=b_blocks, c_blocks=c_blocks, scores=scores)
    )
    outs_heads, finals, gains = lax.map(per_head, (head_signal, head_decay))
    return (outs_heads.transpose(1, 2, 0, 3).reshape(tokens, head_count * HEADDIM), finals, gains)


def carry_terms(decays, c_rows, incoming):
    tokens, head_count = decays.shape
    running_log = jnp.cumsum(decays, axis=0)
    project = jnp.einsum("tn,hpn->thp", c_rows, incoming, precision=HIGHEST_PRECISION)
    return (jnp.exp(running_log)[:, :, None] * project).reshape(tokens, head_count * HEADDIM)


def combine(earlier, later):
    early_gain, early_state = earlier
    late_gain, late_state = later
    return (early_gain * late_gain, late_gain[:, None, None] * early_state + late_state)


def shards(inputs, log_decay, b_proj, c_proj, grad_out):
    signal = inputs.astype(jnp.float32)
    b_rows = b_proj.astype(jnp.float32)
    c_rows = c_proj.astype(jnp.float32)
    upstream = grad_out.astype(jnp.float32)
    scores = score_blocks(b_proj, c_proj)
    head_count = log_decay.shape[1]
    identity = (
        jnp.ones((head_count,), jnp.float32),
        jnp.zeros((head_count, HEADDIM, STATE), jnp.float32),
    )
    (local_out, finals, gains), pull_local = jax.vjp(
        device_terms, signal, log_decay, b_rows, c_rows, scores
    )
    incoming = entering((gains, finals), "seq", combine, identity, False)[1]
    carry_out, pull_carry = jax.vjp(carry_terms, log_decay, c_rows, incoming)
    decay_carry, c_carry, incoming_grad = pull_carry(upstream)
    adjoint = entering((gains, incoming_grad), "seq", combine, identity, True)[1]
    gain_grad = jnp.sum(adjoint * incoming, axis=(1, 2))
    grad_signal, decay_local, b_local, c_local, scores_local = pull_local(
        (upstream, adjoint, gain_grad)
    )
    b_score, c_score = score_grads(scores_local, b_proj, c_proj)
    grad_b, grad_c = lax.psum((b_local + b_score, c_local + c_carry + c_score), "head")
    grad_decay = decay_local + decay_carry
    outputs = (local_out + carry_out).astype(jnp.bfloat16)
    return (outputs, grad_signal.astype(jnp.bfloat16), grad_decay, grad_b, grad_c)


def solution(mesh):
    placed = (P("seq", "head"), P("seq", "head"), P("seq", None), P("seq", None), P("seq", "head"))
    return jax.shard_map(
        shards,
        mesh=mesh,
        in_specs=placed,
        out_specs=(
            P("seq", "head"),
            P("seq", "head"),
            P("seq", "head"),
            P("seq", None),
            P("seq", None),
        ),
        check_vma=False,
    )
```

profile of v0, /device:TPU:1, one launch (start us, length us, event | category | flops | bytes accessed | tf_op | source)
XLA Modules:
  0.0 822.2 jit_solution(16425692722080866038)
XLA Ops:
  11.3 55.9 %while.73 = (s32[]{:T(128)}, f32[10,1,256,64]{2,3,1,0:T(8,128)}, f32[10,64,128]{2,1,0:T(8,128)S(1)}, f32[10]{0:T(128)S(1)}, f32[10,1,256]{2,1,0:T(1,128)S(1)}, /...) while((s32[]{:T(128)}, f32[10,1,256,64]{2,3,1,0:T(8,128)}, ...), condition=%wide.region_3.4_spmd.clone.clone.clone, body=%wide.region_0.3_spmd.clone.clone.sunk.clone | while | flops 13099271 | bytes 1030905 | solution.py:95
  70.7 2.0 fusion.76
  75.0 124.0 %all-reduce.2 = f32[640]{0:T(1024)S(1)} all-reduce(f32[640]{0:T(1024)S(1)} %dynamic-update-slice), channel_id=2, replica_groups=mesh['seq'=64,'head'=8] {'seq'}, use_global_device_ids=true, to_apply=%add.2 | all-reduce | flops 640 | bytes 5120
  200.7 91.5 %all-gather.6.cloned.1.call-done = f32[640,64,128]{2,1,0:T(8,128)} async-done(((f32[10,64,128]{2,1,0:T(8,128)}), f32[640,64,128]{2,1,0:T(8,128)}) %all-gather.6.cloned.1.call-update) | async-done | bytes 20971536 | tf_op jit(solution)/shard_map/all_gather | solution.py:20
  292.3 218.4 %all-gather.8.cloned.1.call-done = f32[640,64,128]{2,1,0:T(8,128)} async-done(((f32[10,64,128]{2,1,0:T(8,128)}), f32[640,64,128]{2,1,0:T(8,128)}) %all-gather.8.cloned.1.call-update) | async-done | bytes 20971536 | tf_op jit(solution)/shard_map/all_gather | solution.py:20
  510.7 71.8 %while.72 = (s32[]{:T(128)}, f32[10,64,128]{2,1,0:T(8,128)S(1)}, s32[]{:T(128)}, f32[64,10]{1,0:T(8,128)S(1)}, f32[64,10,64,128]{3,2,1,0:T(8,128)}) while((s32[]{:T(128)}, f32[10,64,128]{2,1,0:T(8,128)S(1)}, s32[]{:T(128)}, f32[64,10]{1,0:T(8,128)S(1)}, f32[64,10,64,128]{3,2,1,0:T(8,128)}) %tuple.188), condition=%wide.region_9.10_spmd.clone, body=%wide.region_8.9_spmd.sunk.clone | while | flops 163846 | bytes 983275 | solution.py:29
  583.2 154.6 %while.74 = (s32[]{:T(128)}, f32[1,256,256]{2,1,0:T(8,128)}, f32[1,256,128]{1,2,0:T(8,128)S(1)}, f32[1,256,128]{2,1,0:T(8,128)S(1)}, bf16[10,1,256,64]{2,3,1,0:T...) while((s32[]{:T(128)}, f32[1,256,256]{2,1,0:T(8,128)}, ...), condition=%wide.region_22.23_spmd.clone.clone, body=%wide.region_11.22_spmd.clone.sunk.clone | while | flops 77450240 | bytes 2894233 | solution.py:95
  590.1 1.9 fusion.172
  605.5 2.0 fusion.172
  621.0 2.0 fusion.172
  636.5 2.0 fusion.172
  642.5 1.8 fusion.175
  651.9 2.0 fusion.172
  667.4 2.0 fusion.172
  682.9 2.0 fusion.172
  688.9 1.8 fusion.175
  698.3 2.0 fusion.172
  704.4 1.8 fusion.175
  713.8 2.0 fusion.172
  729.3 2.0 fusion.172
  740.9 1.8 convolution_add_fusion.3
  742.8 2.5 reduce-window.80
  745.5 1.9 copy.47
  750.1 62.4 %all-reduce.6.cloned.1.call-done = (f32[256,128]{1,0:T(8,128)}, f32[256,128]{1,0:T(8,128)}) async-done(((f32[256,128]{1,0:T(8,128)}, f32[256,128]{1,0:T(8,128)}), (f32[256,128]{1,0:T(8,128)}, f32[256,128]{1,0:T(8,128)})) %all-reduce.6.cloned.1.call-update) | async-done | bytes 262160 | tf_op jit(solution)/shard_map/psum | solution.py:135
  (626 shorter events, 240.8 us)
Async XLA Ops:
  7.2 575.4 %copy-start = (bf16[256,128]{1,0:T(8,128)(2,1)S(1)}, bf16[256,128]{1,0:T(8,128)(2,1)}, u32[]{:S(2)}) copy-start(bf16[256,128]{1,0:T(8,128)(2,1)} %param.16) | copy-start | bytes 196612
  7.2 285.0 %all-gather.6.cloned.1.call-start = ((), (), s32[]{:S(2)}) async-start(), calls=%async_computation | async-start | bytes 21299200 | tf_op jit(solution)/shard_map/all_gather | solution.py:20
  67.1 0.7 copy-start.1
  67.1 2.4 copy-start.2
  67.9 442.8 %all-gather.8.cloned.1.call-start = ((), (), s32[]{:S(2)}) async-start(), calls=%async_computation.1 | async-start | bytes 21299200 | tf_op jit(solution)/shard_map/all_gather | solution.py:20
  72.8 739.7 %all-reduce.6.cloned.1.call-start = ((), (), s32[]{:S(2)}) async-start(), calls=%async_computation.2 | async-start | bytes 524288 | tf_op jit(solution)/shard_map/psum | solution.py:135
Sparse Core Ops, SparseCore 0:
  68.0 224.1 all-gather.5
  295.2 215.4 all-gather.7
  749.6 62.8 all-reduce.5
where the time goes:
time: 828 us; the launch traced here: 822 us
  waiting for transfers between devices  372 us (45%)
  other arithmetic  140 us (17%)
  blocking collectives  124 us (15%)
  matrix products  86.6 us (10%)
  local copies, waits for them, and re-layouts  48 us (6%)
  loops' own time  37 us (4%)
  between operations  14.6 us (2%)
    all_gather x2, waiting for transfers between devices, entering(): gathered = jax.tree.map(lambda a: lax.all_gather(a, axis), part)  310 us
    unnamed x1, blocking collectives  124 us
    add x63, other arithmetic, combine(): late_gain[:, None, None] * early_state + late_state  68.8 us
    psum x1, waiting for transfers between devices, shards(): lax.psum((b_local + b_score, c_local + c_carry + c_score), 'head')  62.4 us
    dot_general x30, matrix products, block_terms(): jnp.einsum('kts,ksp->ktp', weighted, head_signal.astype(jnp.bfloat16), pr...  46.9 us
    another operation x2, loops' own time, device_terms(): outs_heads, finals, gains = lax.map(per_head, (head_signal, head_decay))  34.6 us
    another operation x77, other arithmetic  27.4 us
    dot_general x30, matrix products, block_terms(): jnp.einsum('ksp,ksn->kpn', scaled, b_blocks.astype(jnp.bfloat16), preferr...  23.3 us
  transfers between devices with their start and end apart: 3, of which 3 were waited for; matrix products, arithmetic and copies ran while one was open for 1% of the time, Pallas kernels for 0%

commit v1 on v0

v1 whole, which is shorter than its diff:
```python
import functools

import jax
import jax.numpy as jnp
from jax import lax
from jax.experimental import pallas as pl
from jax.experimental.pallas import tpu as pltpu
from jax.sharding import PartitionSpec as P

HEADDIM = 64
STATE = 128
PAIR = 128
HALF = 64
MSG = HALF + 8
GROUP = 4
MESH = pl.DeviceIdType.MESH
F32 = jnp.float32
BF16 = jnp.bfloat16
VMEM = pltpu.MemorySpace.VMEM
HIGHEST = lax.Precision.HIGHEST


def dot(a, b, da=1, db=0, precision=None):
    return lax.dot_general(
        a, b, (((da,), (db,)), ((), ())), precision=precision, preferred_element_type=F32
    )


def split_dot(a, b):
    high = a.astype(BF16)
    low = (a - high.astype(F32)).astype(BF16)
    return dot(high, b) + dot(low, b)


def lower(n, strict=False):
    r = lax.broadcasted_iota(jnp.int32, (n, n), 0)
    c = lax.broadcasted_iota(jnp.int32, (n, n), 1)
    return r > c if strict else r >= c


def head_of_lane(heads, lanes):
    r = lax.broadcasted_iota(jnp.int32, (heads, lanes), 0)
    c = lax.broadcasted_iota(jnp.int32, (heads, lanes), 1)
    return jnp.where(c // HEADDIM == r, 1.0, 0.0).astype(BF16)


def lane_head(lanes, heads):
    r = lax.broadcasted_iota(jnp.int32, (lanes, heads), 0)
    c = lax.broadcasted_iota(jnp.int32, (lanes, heads), 1)
    return jnp.where(r // HEADDIM == c, 1.0, 0.0).astype(BF16)


def decays(ld):
    tokens, heads = ld.shape
    prefix = dot(lower(tokens).astype(F32), ld, precision=HIGHEST)
    spread = head_of_lane(heads, heads * HEADDIM)
    grown = split_dot(jnp.exp(prefix), spread)
    left = split_dot(jnp.exp(prefix[tokens - 1 : tokens] - prefix), spread)
    return prefix, grown, left


def local_kernel(x_ref, ld_ref, b_ref, c_ref, g_ref, sf_ref, sb_ref, within_ref, dxw_ref, gb_ref, gc_ref):
    tokens, heads = ld_ref.shape
    ld = ld_ref[...]
    prefix, grown, left = decays(ld)
    rows = dot(ld, lower(tokens).astype(F32), 0, 1, precision=HIGHEST)
    b, c = b_ref[...], c_ref[...]
    scaled = (x_ref[...].astype(F32) * left).astype(BF16)
    risen = (g_ref[...].astype(F32) * grown).astype(BF16)
    states = dot(b, scaled, 0, 0)
    pulls = dot(c, risen, 0, 0)
    gain = grown[tokens - 1 : tokens]
    for ch in range(heads):
        j, half = ch // 2, ch % 2
        lanes = slice(j * PAIR, (j + 1) * PAIR)
        span = slice(half * HALF, (half + 1) * HALF)
        tile = jnp.broadcast_to(gain[:, lanes], (8, PAIR))
        sf_ref[ch, :HALF] = states[span, lanes]
        sf_ref[ch, HALF:] = tile
        sb_ref[ch, :HALF] = pulls[span, lanes]
        sb_ref[ch, HALF:] = tile
    scores = dot(c, b, 1, 1)
    causal = lower(tokens)
    first = lax.broadcasted_iota(jnp.int32, (tokens, PAIR), 1) < HEADDIM
    total = jnp.zeros((tokens, tokens), F32)
    for j in range(heads // 2):
        lanes = slice(j * PAIR, (j + 1) * PAIR)
        xp, gp = x_ref[:, lanes], g_ref[:, lanes]
        parts = []
        for e in range(2):
            h = 2 * j + e
            decay = jnp.where(causal, jnp.exp(prefix[:, h : h + 1] - rows[h : h + 1]), 0.0)
            weighted = (scores * decay).astype(BF16)
            own = jnp.where(first if e == 0 else ~first, gp.astype(F32), 0.0).astype(BF16)
            total += dot(own, xp, 1, 1) * decay
            parts.append((dot(weighted, xp), dot(weighted, gp, 0, 0)))
        within_ref[:, lanes] = jnp.where(first, parts[0][0], parts[1][0])
        dxw_ref[:, lanes] = jnp.where(first, parts[0][1], parts[1][1])
    halved = total.astype(BF16)
    gc_ref[...] = dot(halved, b)
    gb_ref[...] = dot(halved, c, 0, 0)


def after_kernel(
    x_ref, ld_ref, b_ref, c_ref, g_ref, within_ref, dxw_ref, gb_ref, gc_ref, start_ref, adj_ref,
    out_ref, dx_ref, dld_ref, both_ref,
):
    tokens, heads = ld_ref.shape
    prefix, grown, left = decays(ld_ref[...])
    b, c = b_ref[...], c_ref[...]
    gain = grown[tokens - 1 : tokens]
    spread = lane_head(heads * HEADDIM, heads)
    gb, gc = gb_ref[...], gc_ref[...]
    rising = jnp.zeros((tokens, heads), F32)
    falling = jnp.zeros((tokens, heads), F32)
    last = jnp.zeros((8, heads), F32)
    for j in range(heads // 2):
        lanes = slice(j * PAIR, (j + 1) * PAIR)
        x, g = x_ref[:, lanes].astype(F32), g_ref[:, lanes].astype(F32)
        start = jnp.concatenate([start_ref[2 * j], start_ref[2 * j + 1]], axis=0)
        adj = jnp.concatenate([adj_ref[2 * j], adj_ref[2 * j + 1]], axis=0)
        start16, adj16 = start.astype(BF16), adj.astype(BF16)
        own = spread[lanes]
        out = within_ref[:, lanes] + grown[:, lanes] * dot(c, start16)
        pushed = left[:, lanes] * dot(b, adj16)
        out_ref[:, lanes] = out.astype(BF16)
        dx_ref[:, lanes] = (dxw_ref[:, lanes] + pushed).astype(BF16)
        gc += dot((g * grown[:, lanes]).astype(BF16), start16, 1, 1)
        gb += dot((x * left[:, lanes]).astype(BF16), adj16, 1, 1)
        rising += split_dot(g * out - x * dxw_ref[:, lanes], own)
        falling += split_dot(x * pushed, own)
        meet = jnp.sum(start * adj, axis=0, keepdims=True) * gain[:, lanes]
        last += split_dot(jnp.broadcast_to(meet, (8, PAIR)), own)
    dld_ref[...] = (
        dot(lower(tokens).astype(F32), rising, 0, 0, precision=HIGHEST)
        + dot(lower(tokens, True).astype(F32), falling, precision=HIGHEST)
        + last[:1]
    )
    both_ref[:tokens] = gb
    both_ref[tokens:] = gc


def carry_kernel(
    sf_ref, sb_ref, start_ref, adj_ref,
    own_in, up_in, up_out, at_owner, from_owner, down_in, down_out,
    up_send, up_recv, own_recv, own_send, down_recv, down_send, rep_send,
):
    chunks = sf_ref.shape[0]
    groups = lax.axis_size("seq") // GROUP
    seq, head = lax.axis_index("seq"), lax.axis_index("head")
    group, place = seq // GROUP, lax.rem(seq, GROUP)
    shift = lax.rem(head, 2) * chunks
    outer = (place == 0) | (place == GROUP - 1)
    early = jnp.where(place < GROUP // 2, 0, 1)
    late = 1 - early
    ahead = jnp.where(early == 0, 1, -1)

    def owner(scan, ch):
        where = lax.rem(ch + shift, groups)
        return (jnp.where(scan == 0, where * GROUP + 1, (groups - 1 - where) * GROUP + 2), head)

    mine = lax.rem(group - shift + 2 * groups, groups)
    mine = jnp.where(place == 1, mine, lax.rem(groups - 1 - group - shift + 2 * groups, groups))
    owns = ~outer & (mine < chunks)
    scan_owned = place - 1

    barrier = pltpu.get_barrier_semaphore()

    def greet(where):
        pl.semaphore_signal(barrier, inc=1, device_id=where, device_id_type=MESH)

    @pl.when(outer)
    def _():
        greet((seq + ahead, head))

        def both(ch, _):
            greet(owner(0, ch))
            greet(owner(1, ch))
            return 0

        lax.fori_loop(0, chunks, both, 0)
        pl.semaphore_wait(barrier, 2 * chunks + 1)

    @pl.when(~outer)
    def _():
        greet((seq + 1, head))
        greet((seq - 1, head))

        @pl.when(owns)
        def _():
            def each(k, _):
                greet((k * GROUP, head))
                greet((k * GROUP + GROUP - 1, head))
                return 0

            lax.fori_loop(0, groups, each, 0)
            pl.semaphore_wait(barrier, 2 * groups + 2)

        @pl.when(~owns)
        def _():
            pl.semaphore_wait(barrier, 2)

    own_in[0] = sf_ref[...]
    own_in[1] = sb_ref[...]

    def up_copy(scan, ch, source, to):
        return pltpu.make_async_remote_copy(
            src_ref=source, dst_ref=up_in.at[scan, ch], send_sem=up_send.at[scan, ch],
            recv_sem=up_recv.at[scan, ch], device_id=to, device_id_type=MESH,
        )

    def down_copy(scan, ch, to):
        return pltpu.make_async_remote_copy(
            src_ref=down_out.at[scan, ch], dst_ref=down_in.at[scan, ch], send_sem=down_send.at[scan, ch],
            recv_sem=down_recv.at[scan, ch], device_id=to, device_id_type=MESH,
        )

    def owner_copy(scan, ch):
        k = jnp.where(scan == 0, group, groups - 1 - group)
        return pltpu.make_async_remote_copy(
            src_ref=up_out.at[scan, ch], dst_ref=at_owner.at[k], send_sem=rep_send.at[ch],
            recv_sem=own_recv.at[k], device_id=owner(scan, ch), device_id_type=MESH,
        )

    def back_copy(k):
        to = jnp.where(scan_owned == 0, k * GROUP, (groups - 1 - k) * GROUP + GROUP - 1)
        return pltpu.make_async_remote_copy(
            src_ref=from_owner.at[k], dst_ref=down_in.at[scan_owned, mine], send_sem=own_send.at[k],
            recv_sem=down_recv.at[scan_owned, mine], device_id=(to, head), device_id_type=MESH,
        )

    e_to, l_to = (seq + ahead, head), (seq - ahead, head)

    def rise(scan, ch):
        gain = own_in[scan, ch, HALF:]
        carried = up_in[scan, ch, HALF:]
        up_out[scan, ch, :HALF] = own_in[scan, ch, :HALF] + gain[:1] * up_in[scan, ch, :HALF]
        up_out[scan, ch, HALF:] = gain * carried

    def up_wait(scan, ch):
        up_copy(scan, ch, up_out.at[scan, ch], e_to).wait_recv()

    @pl.when(outer)
    def _():
        def send(ch, _):
            up_copy(early, ch, own_in.at[early, ch], e_to).start()
            return 0

        lax.fori_loop(0, chunks, send, 0)

        def total(ch, _):
            up_wait(late, ch)
            rise(late, ch)
            owner_copy(late, ch).start()
            return 0

        lax.fori_loop(0, chunks, total, 0)

    lag = min(4, chunks)

    @pl.when(~outer)
    def _():
        def step(i, _):
            @pl.when(i < chunks)
            def _():
                up_wait(early, i)
                rise(early, i)
                up_copy(early, i, up_out.at[early, i], e_to).start()

            @pl.when(i >= lag)
            def _():
                ch = i - lag
                up_wait(late, ch)
                rise(late, ch)
                up_copy(late, ch, up_out.at[late, ch], l_to).start()

            return 0

        lax.fori_loop(0, chunks + lag, step, 0)

    @pl.when(owns)
    def _():
        def scan_groups(k, carry):
            from_owner[k] = carry
            back_copy(k).start()
            pltpu.make_async_remote_copy(
                src_ref=at_owner.at[k], dst_ref=at_owner.at[k], send_sem=own_send.at[k],
                recv_sem=own_recv.at[k], device_id=(seq + 1, head), device_id_type=MESH,
            ).wait_recv()
            return at_owner[k, HALF : HALF + 1] * carry + at_owner[k, :HALF]

        lax.fori_loop(0, groups, scan_groups, jnp.zeros((HALF, PAIR), F32))

    def down_wait(scan, ch):
        down_copy(scan, ch, e_to).wait_recv()

    def fall(scan, ch):
        down_out[scan, ch] = (
            own_in[scan, ch, :HALF] + own_in[scan, ch, HALF : HALF + 1] * down_in[scan, ch]
        )

    @pl.when(outer)
    def _():
        def step(i, _):
            @pl.when(i < chunks)
            def _():
                down_wait(early, i)
                fall(early, i)
                down_copy(early, i, e_to).start()

            return 0

        lax.fori_loop(0, chunks, step, 0)

        def end(ch, _):
            down_wait(late, ch)
            return 0

        lax.fori_loop(0, chunks, end, 0)

    @pl.when(~outer)
    def _():
        def step(i, _):
            @pl.when(i < chunks)
            def _():
                down_wait(early, i)
                fall(early, i)
                down_copy(early, i, e_to).start()

            @pl.when(i >= lag)
            def _():
                ch = i - lag
                down_wait(late, ch)
                fall(late, ch)
                down_copy(late, ch, l_to).start()

            return 0

        lax.fori_loop(0, chunks + lag, step, 0)

    start_ref[...] = down_in[0]
    adj_ref[...] = down_in[1]

    def left(ch, _):
        up_copy(early, ch, up_out.at[early, ch], e_to).wait_send()
        down_copy(early, ch, e_to).wait_send()

        @pl.when(outer)
        def _():
            owner_copy(late, ch).wait_send()

        @pl.when(~outer)
        def _():
            up_copy(late, ch, up_out.at[late, ch], l_to).wait_send()
            down_copy(late, ch, l_to).wait_send()

        return 0

    lax.fori_loop(0, chunks, left, 0)

    @pl.when(owns)
    def _():
        def sent(k, _):
            back_copy(k).wait_send()
            return 0

        lax.fori_loop(0, groups, sent, 0)


def carry(sf, sb):
    chunks = sf.shape[0]
    groups = lax.axis_size("seq") // GROUP
    state = jax.ShapeDtypeStruct((chunks, HALF, PAIR), F32)
    dma = pltpu.SemaphoreType.DMA
    return pl.pallas_call(
        carry_kernel,
        out_shape=(state, state),
        in_specs=[pl.BlockSpec(memory_space=VMEM)] * 2,
        out_specs=(pl.BlockSpec(memory_space=VMEM),) * 2,
        scratch_shapes=[
            pltpu.VMEM((2, chunks, MSG, PAIR), F32),
            pltpu.VMEM((2, chunks, MSG, PAIR), F32),
            pltpu.VMEM((2, chunks, MSG, PAIR), F32),
            pltpu.VMEM((groups, MSG, PAIR), F32),
            pltpu.VMEM((groups, HALF, PAIR), F32),
            pltpu.VMEM((2, chunks, HALF, PAIR), F32),
            pltpu.VMEM((2, chunks, HALF, PAIR), F32),
            dma((2, chunks)), dma((2, chunks)), dma((groups,)), dma((groups,)),
            dma((2, chunks)), dma((2, chunks)), dma((chunks,)),
        ],
        compiler_params=pltpu.CompilerParams(
            collective_id=0, has_side_effects=True, vmem_limit_bytes=48 * 2**20
        ),
        name="carry",
    )(sf, sb)


def sum_kernel(n, both_ref, sum_ref, parts, done, part_send, part_recv, done_send, done_recv):
    seq, head = lax.axis_index("seq"), lax.axis_index("head")
    rows = both_ref.shape[0] // n
    barrier = pltpu.get_barrier_semaphore()
    for step in range(1, n):
        pl.semaphore_signal(
            barrier, inc=1, device_id=(seq, lax.rem(head + step, n)), device_id_type=MESH
        )
    pl.semaphore_wait(barrier, n - 1)

    def part(step):
        to = lax.rem(head + step, n)
        return pltpu.make_async_remote_copy(
            src_ref=both_ref.at[pl.ds(pl.multiple_of(to * rows, rows), rows)], dst_ref=parts.at[step],
            send_sem=part_send.at[step], recv_sem=part_recv.at[step],
            device_id=(seq, to), device_id_type=MESH,
        )

    def whole(step):
        to = lax.rem(head + step, n)
        here = pl.ds(pl.multiple_of(head * rows, rows), rows)
        return pltpu.make_async_remote_copy(
            src_ref=done.at[here], dst_ref=done.at[here], send_sem=done_send.at[step],
            recv_sem=done_recv.at[step], device_id=(seq, to), device_id_type=MESH,
        )

    for step in range(1, n):
        part(step).start()
    here = pl.ds(pl.multiple_of(head * rows, rows), rows)
    total = both_ref[here]
    for step in range(1, n):
        part(step).wait_recv()
        total += parts[step]
    done[here] = total
    for step in range(1, n):
        whole(step).start()
    for step in range(1, n):
        part(step).wait_send()
    for step in range(1, n):
        whole(step).wait()
    sum_ref[...] = done[...]


def summed(both):
    n = lax.axis_size("head")
    rows, columns = both.shape
    dma = pltpu.SemaphoreType.DMA
    return pl.pallas_call(
        functools.partial(sum_kernel, n),
        out_shape=jax.ShapeDtypeStruct(both.shape, F32),
        in_specs=[pl.BlockSpec(memory_space=VMEM)],
        out_specs=pl.BlockSpec(memory_space=VMEM),
        scratch_shapes=[
            pltpu.VMEM((n, rows // n, columns), F32),
            pltpu.VMEM((rows, columns), F32),
            dma((n,)), dma((n,)), dma((n,)), dma((n,)),
        ],
        compiler_params=pltpu.CompilerParams(collective_id=1, has_side_effects=True),
        name="summed",
    )(both)


def shards(inputs, log_decay, b_proj, c_proj, grad_out):
    tokens, heads = log_decay.shape
    wide = jax.ShapeDtypeStruct(inputs.shape, F32)
    thin = jax.ShapeDtypeStruct((tokens, STATE), F32)
    message = jax.ShapeDtypeStruct((heads, MSG, PAIR), F32)
    whole = pl.BlockSpec(memory_space=VMEM)
    room = pltpu.CompilerParams(vmem_limit_bytes=48 * 2**20)
    sf, sb, within, dxw, gb, gc = pl.pallas_call(
        local_kernel,
        out_shape=(message, message, wide, wide, thin, thin),
        in_specs=[whole] * 5, out_specs=(whole,) * 6, compiler_params=room, name="local",
    )(inputs, log_decay, b_proj, c_proj, grad_out)
    start, adj = carry(sf, sb)
    outputs, grad_inputs, grad_decay, both = pl.pallas_call(
        after_kernel,
        out_shape=(
            jax.ShapeDtypeStruct(inputs.shape, BF16),
            jax.ShapeDtypeStruct(inputs.shape, BF16),
            jax.ShapeDtypeStruct(log_decay.shape, F32),
            jax.ShapeDtypeStruct((2 * tokens, STATE), F32),
        ),
        in_specs=[whole] * 11, out_specs=(whole,) * 4, compiler_params=room, name="after",
    )(inputs, log_decay, b_proj, c_proj, grad_out, within, dxw, gb, gc, start, adj)
    both = summed(both)
    return outputs, grad_inputs, grad_decay, both[:tokens], both[tokens:]


def solution(mesh):
    placed = (P("seq", "head"), P("seq", "head"), P("seq", None), P("seq", None), P("seq", "head"))
    return jax.shard_map(
        shards,
        mesh=mesh,
        in_specs=placed,
        out_specs=(
            P("seq", "head"),
            P("seq", "head"),
            P("seq", "head"),
            P("seq", None),
            P("seq", None),
        ),
        check_vma=False,
    )
```

time: 828 us -> 103 us (0.12)
  waiting for transfers between devices: 372 us -> 0 us
  other arithmetic: 140 us -> 0 us
  blocking collectives: 124 us -> 0 us
  Pallas kernels: 0 us -> 95.7 us
  matrix products: 86.6 us -> 0 us
  local copies, waits for them, and re-layouts: 48 us -> 5.91 us
  loops' own time: 37 us -> 0 us
  between operations: 14.6 us -> 0.72 us
    all_gather x2 -> x0, waiting for transfers between devices: 310 us -> none  [entering(): gathered = jax.tree.map(lambda a: lax.all_gather(a, axis), part)]
    unnamed x1 -> x0, blocking collectives: 124 us -> none
    pallas_call x0 -> x4, Pallas kernels: none -> 95.7 us  [the longest x1 63.6 us: carry(): pl.pallas_call(carry_kernel, out_shape=(state, state), in_specs=[pl.Block...]
    dot_general x87 -> x0, matrix products: 86.6 us -> none  [the longest x30 46.9 us: block_terms(): jnp.einsum('kts,ksp->ktp', weighted, head_signal.astype(jnp.bfloat16), pr...]
    add x64 -> x0, other arithmetic: 69.4 us -> none  [the longest x63 68.8 us: combine(): late_gain[:, None, None] * early_state + late_state]
    psum x1 -> x0, waiting for transfers between devices: 62.4 us -> none  [shards(): lax.psum((b_local + b_score, c_local + c_carry + c_score), 'head')]
    another operation x4 -> x0, loops' own time: 37 us -> none  [the longest x2 34.6 us: device_terms(): outs_heads, finals, gains = lax.map(per_head, (head_signal, head_decay))]
    another operation x77 -> x0, other arithmetic: 27.4 us -> none
  transfers between devices with their start and end apart: 3 -> 0, of which waited for: 3 -> 0; matrix products, arithmetic and copies ran while one was open for 1% -> 0% of each run, Pallas kernels for 0% -> 0%
where the time goes in v1:
time: 103 us; the launch traced here: 102 us
  Pallas kernels  95.7 us (93%)
  local copies, waits for them, and re-layouts  5.91 us (6%)
    pallas_call x1, Pallas kernels, carry(): pl.pallas_call(carry_kernel, out_shape=(state, state), in_specs=[pl.Block...  63.6 us
    pallas_call x1, Pallas kernels, summed(): pl.pallas_call(functools.partial(sum_kernel, n), out_shape=jax.ShapeDtype...  26.2 us
    unnamed x16, local copies, waits for them, and re-layouts  4.22 us
    pallas_call x1, Pallas kernels, shards(): pl.pallas_call(after_kernel, out_shape=(jax.ShapeDtypeStruct(inputs.shape...  3.01 us
    pallas_call x1, Pallas kernels, shards(): pl.pallas_call(local_kernel, out_shape=(message, message, wide, wide, thi...  2.95 us

profile of v1, /device:TPU:1, one launch (start us, length us, event | category | flops | bytes accessed | tf_op | source)
XLA Modules:
  0.0 102.4 jit_solution(5242552236065610205)
XLA Ops:
  0.6 0.0 copy-start.5
  0.6 0.0 copy-start.4
  0.7 0.9 copy.11.ld_ref
  1.5 0.0 copy-done.5
  1.5 0.0 copy-done.4
  1.5 0.0 copy-start
  1.5 1.0 copy-done
  2.5 0.0 copy-start.2
  2.5 1.0 copy-done.2
  3.5 2.9 %local.1 = (f32[10,72,128]{2,1,0:T(8,128)S(1)}, f32[10,72,128]{2,1,0:T(8,128)S(1)}, f32[256,640]{1,0:T(8,128)S(1)}, f32[256,640]{1,0:T(8,128)S(1)}, f32[256,128]{1,0:T(8,128)S(1)}, /*index=5*/f32[256,128]{1,0:T(8,128)S(1)}) custom-call(bf16[256,640]{1,0:T(8,128)(2,1)S(1)} %copy-done, f32[256,10]{1,0:T(8,128)S(1)} %copy.11.ld_ref, ...), custom_call_target="tpu_custom_call" | custom-call | tf_op jit(solution)/shard_map/local/pallas_call | solution.py:467
  6.4 0.0 copy-start.1
  6.4 0.0 copy-start.3
  6.5 63.6 %carry.1 = (f32[10,64,128]{2,1,0:T(8,128)S(1)}, f32[10,64,128]{2,1,0:T(8,128)S(1)}) custom-call(f32[10,72,128]{2,1,0:T(8,128)S(1)} %get-tuple-element.21.sf_ref, f32[10,72,128]{2,1,0:T(8,128)S(1)} %get-tuple-element.22.sb_ref), custom_call_target="tpu_custom_call" | custom-call | tf_op jit(solution)/shard_map/carry/pallas_call | solution.py:375
  70.1 0.0 copy-done.1
  70.1 0.0 copy-done.3
  70.1 3.0 %after.1 = (bf16[256,640]{1,0:T(8,128)(2,1)}, bf16[256,640]{1,0:T(8,128)(2,1)}, f32[256,10]{1,0:T(8,128)S(1)}, f32[512,128]{1,0:T(8,128)S(1)}) custom-call(bf16[256,640]{1,0:T(8,128)(2,1)S(1)} %copy-done.1, f32[256,10]{1,0:T(8,128)S(1)} %copy.11.ld_ref, bf16[256,128]{1,0:T(8,128)(2,1)S(1)} %copy-done.4, bf16[256,128]{1,0:T(8,128)(2,1)S(1)} %copy-done.5, ...), custom_call_target="tpu_custom_call" | custom-call | tf_op jit(solution)/shard_map/after/pallas_call | solution.py:473
  73.1 0.0 copy-start.6
  73.1 0.7 copy-done.6
  73.8 0.7 copy.12
  74.5 26.2 %summed.1 = f32[512,128]{1,0:T(8,128)} custom-call(f32[512,128]{1,0:T(8,128)} %copy-done.6), custom_call_target="tpu_custom_call" | custom-call | tf_op jit(solution)/shard_map/summed/pallas_call | solution.py:445
  100.7 1.7 %fusion = (f32[256,128]{1,0:T(8,128)}, f32[256,128]{1,0:T(8,128)}) fusion(f32[512,128]{1,0:T(8,128)} %summed.1), kind=kLoop, calls=%fused_computation | loop fusion | bytes 524288 | tf_op jit(solution)/shard_map/slice | solution.py:484
Async XLA Ops:
  0.6 0.9 copy-start.5
  0.6 0.9 copy-start.4
  1.5 1.0 copy-start
  2.5 1.0 copy-start.2
  6.4 63.6 %copy-start.1 = (bf16[256,640]{1,0:T(8,128)(2,1)S(1)}, bf16[256,640]{1,0:T(8,128)(2,1)}, u32[]{:S(2)}) copy-start(bf16[256,640]{1,0:T(8,128)(2,1)} %x_ref.3) | copy-start | bytes 983044
  6.4 63.6 %copy-start.3 = (bf16[256,640]{1,0:T(8,128)(2,1)S(1)}, bf16[256,640]{1,0:T(8,128)(2,1)}, u32[]{:S(2)}) copy-start(bf16[256,640]{1,0:T(8,128)(2,1)} %g_ref.3) | copy-start | bytes 983044
  73.1 0.7 copy-start.6

commit v2 on v0

v2 whole, which is shorter than its diff:
```python
import jax
import jax.numpy as jnp
from jax import lax
from jax.experimental import pallas as pl
from jax.experimental.pallas import tpu as pltpu
from jax.sharding import PartitionSpec as P

HEADDIM = 64
STATE = 128
PAIR = 128
GROUP = 4
LAG = 5
MESH = pl.DeviceIdType.MESH
F32 = jnp.float32
BF16 = jnp.bfloat16
VMEM = pltpu.MemorySpace.VMEM
HIGHEST = lax.Precision.HIGHEST


def dot(a, b, da=1, db=0, precision=None):
    return lax.dot_general(
        a, b, (((da,), (db,)), ((), ())), precision=precision, preferred_element_type=F32
    )


def split_dot(a, b):
    high = a.astype(BF16)
    low = (a - high.astype(F32)).astype(BF16)
    return dot(high, b) + dot(low, b)


def lower(n, strict=False):
    r = lax.broadcasted_iota(jnp.int32, (n, n), 0)
    c = lax.broadcasted_iota(jnp.int32, (n, n), 1)
    return r > c if strict else r >= c


def head_of_lane(heads, lanes):
    r = lax.broadcasted_iota(jnp.int32, (heads, lanes), 0)
    c = lax.broadcasted_iota(jnp.int32, (heads, lanes), 1)
    return jnp.where(c // HEADDIM == r, 1.0, 0.0).astype(BF16)


def lane_head(lanes, heads):
    r = lax.broadcasted_iota(jnp.int32, (lanes, heads), 0)
    c = lax.broadcasted_iota(jnp.int32, (lanes, heads), 1)
    return jnp.where(r // HEADDIM == c, 1.0, 0.0).astype(BF16)


def decays(ldt):
    heads, tokens = ldt.shape
    prefix = dot(lower(tokens).astype(F32), ldt, 1, 1, precision=HIGHEST)
    spread = head_of_lane(heads, heads * HEADDIM)
    grown = split_dot(jnp.exp(prefix), spread)
    left = split_dot(jnp.exp(prefix[tokens - 1 : tokens] - prefix), spread)
    return prefix, grown, left


def main_kernel(
    x_ref, ldt_ref, b_ref, c_ref, g_ref, out_ref, dx_ref, dldt_ref, gb_ref, gc_ref,
    grown_ref, left_ref, within_ref, dxw_ref, factor, grads,
    own_in, up_in, up_out, down_in, down_out, at_owner, from_owner,
    gain_own, gain_in, gain_out, gain_at, unit_out, unit_in, full,
    up_send, up_recv, own_recv, own_send, down_recv, down_send, rep_send,
    gain_send, gain_recv, gain_far_send, gain_far_recv, unit_send, unit_recv, full_send, full_recv,
):
    heads, tokens = ldt_ref.shape
    lanes = heads * HEADDIM
    pairs = lanes // PAIR
    groups = lax.axis_size("seq") // GROUP
    peers = lax.axis_size("head")
    chunks = groups
    deep = STATE // chunks
    parts = peers // 2
    per = chunks // parts
    wide = STATE // parts
    seq, head = lax.axis_index("seq"), lax.axis_index("head")
    group, place = seq // GROUP, lax.rem(seq, GROUP)
    shift = lax.rem(head, 2) * (groups // 2)
    outer = (place == 0) | (place == GROUP - 1)
    early = jnp.where(place < GROUP // 2, 0, 1)
    late = 1 - early
    ahead = jnp.where(early == 0, 1, -1)
    e_to, l_to = (seq + ahead, head), (seq - ahead, head)

    def owner(scan, ch):
        where = lax.rem(ch + shift, groups)
        return (jnp.where(scan == 0, where * GROUP + 1, (groups - 1 - where) * GROUP + 2), head)

    scan_owned = jnp.where(place == 1, 0, 1)
    mine = lax.rem(jnp.where(place == 1, group, groups - 1 - group) + groups - shift, groups)

    barrier = pltpu.get_barrier_semaphore()

    def greet(where):
        pl.semaphore_signal(barrier, inc=1, device_id=where, device_id_type=MESH)

    @pl.when(outer)
    def _():
        def each(k, _):
            greet((k * GROUP + 1, head))
            greet((k * GROUP + 2, head))
            return 0

        lax.fori_loop(0, groups, each, 0)

    @pl.when(~outer)
    def _():
        def each(k, _):
            greet((k * GROUP, head))
            greet((k * GROUP + GROUP - 1, head))
            return 0

        lax.fori_loop(0, groups, each, 0)
        greet((jnp.where(place == 1, seq + 1, seq - 1), head))

    for step in range(1, peers):
        greet((seq, lax.rem(head + step, peers)))

    ldt = ldt_ref[...]
    prefix, grown, left = decays(ldt)
    grown_ref[...] = grown
    left_ref[...] = left
    rows = dot(ldt, lower(tokens).astype(F32), 1, 1, precision=HIGHEST)
    b, c = b_ref[...], c_ref[...]
    risen = (g_ref[...].astype(F32) * grown).astype(BF16)
    scaled = (x_ref[...].astype(F32) * left).astype(BF16)
    factor[0] = risen
    factor[1] = scaled
    own_in[0] = dot(b, scaled, 0, 0).reshape(chunks, deep, lanes)
    own_in[1] = dot(c, risen, 0, 0).reshape(chunks, deep, lanes)
    for j in range(pairs):
        gain_own[j : j + 1] = grown[tokens - 1 : tokens, j * PAIR : (j + 1) * PAIR]
    gain_own[pairs:] = jnp.zeros((8 - pairs, PAIR), F32)

    scores = dot(c, b, 1, 1)
    causal = lower(tokens)
    first = lax.broadcasted_iota(jnp.int32, (tokens, PAIR), 1) < HEADDIM
    total = jnp.zeros((tokens, tokens), F32)
    for j in range(pairs):
        span = slice(j * PAIR, (j + 1) * PAIR)
        xp, gp = x_ref[:, span], g_ref[:, span]
        found = []
        for e in range(2):
            h = 2 * j + e
            decay = jnp.where(causal, jnp.exp(prefix[:, h : h + 1] - rows[h : h + 1]), 0.0)
            weighted = (scores * decay).astype(BF16)
            own = jnp.where(first if e == 0 else ~first, gp.astype(F32), 0.0).astype(BF16)
            total += dot(own, xp, 1, 1) * decay
            found.append((dot(weighted, xp), dot(weighted, gp, 0, 0)))
        within_ref[:, span] = jnp.where(first, found[0][0], found[1][0])
        dxw_ref[:, span] = jnp.where(first, found[0][1], found[1][1])
    halved = total.astype(BF16)
    grads[0] = dot(b, halved, 0, 1)
    grads[1] = dot(c, halved, 0, 0)

    @pl.when(outer)
    def _():
        pl.semaphore_wait(barrier, 2 * groups + peers - 1)

    @pl.when(~outer)
    def _():
        pl.semaphore_wait(barrier, 2 * groups + 1 + peers - 1)

    def up_copy(scan, ch, source, to):
        return pltpu.make_async_remote_copy(
            src_ref=source, dst_ref=up_in.at[scan, ch], send_sem=up_send.at[scan, ch],
            recv_sem=up_recv.at[scan, ch], device_id=to, device_id_type=MESH,
        )

    def gain_copy(scan, source, to):
        return pltpu.make_async_remote_copy(
            src_ref=source, dst_ref=gain_in.at[scan], send_sem=gain_send.at[scan],
            recv_sem=gain_recv.at[scan], device_id=to, device_id_type=MESH,
        )

    def down_copy(scan, ch, to):
        return pltpu.make_async_remote_copy(
            src_ref=down_out.at[scan, ch], dst_ref=down_in.at[scan, ch], send_sem=down_send.at[scan, ch],
            recv_sem=down_recv.at[scan, ch], device_id=to, device_id_type=MESH,
        )

    rank = jnp.where(late == 0, group, groups - 1 - group)

    def owner_copy(ch):
        return pltpu.make_async_remote_copy(
            src_ref=up_out.at[late, ch], dst_ref=at_owner.at[rank], send_sem=rep_send.at[ch],
            recv_sem=own_recv.at[rank], device_id=owner(late, ch), device_id_type=MESH,
        )

    def gain_far_copy(ch):
        return pltpu.make_async_remote_copy(
            src_ref=gain_out.at[late], dst_ref=gain_at.at[rank], send_sem=gain_far_send.at[ch],
            recv_sem=gain_far_recv.at[rank], device_id=owner(late, ch), device_id_type=MESH,
        )

    def arrived(buffer, sem, k):
        pltpu.make_async_remote_copy(
            src_ref=buffer.at[k], dst_ref=buffer.at[k], send_sem=own_send.at[k],
            recv_sem=sem.at[k], device_id=e_to, device_id_type=MESH,
        ).wait_recv()

    def back_copy(k):
        to = jnp.where(scan_owned == 0, k * GROUP, (groups - 1 - k) * GROUP + GROUP - 1)
        return pltpu.make_async_remote_copy(
            src_ref=from_owner.at[k], dst_ref=down_in.at[scan_owned, mine], send_sem=own_send.at[k],
            recv_sem=down_recv.at[scan_owned, mine], device_id=(to, head), device_id_type=MESH,
        )

    def unit_copy(u):
        return pltpu.make_async_remote_copy(
            src_ref=unit_out.at[u], dst_ref=unit_in.at[head], send_sem=unit_send.at[u],
            recv_sem=unit_recv.at[head], device_id=(seq, u), device_id_type=MESH,
        )

    def unit_from(u):
        return pltpu.make_async_remote_copy(
            src_ref=unit_in.at[u], dst_ref=unit_in.at[u], send_sem=unit_send.at[u],
            recv_sem=unit_recv.at[u], device_id=(seq, u), device_id_type=MESH,
        )

    def full_copy(u):
        return pltpu.make_async_remote_copy(
            src_ref=full.at[head], dst_ref=full.at[head], send_sem=full_send.at[u],
            recv_sem=full_recv.at[head], device_id=(seq, u), device_id_type=MESH,
        )

    def full_from(u):
        return pltpu.make_async_remote_copy(
            src_ref=full.at[u], dst_ref=full.at[u], send_sem=full_send.at[u],
            recv_sem=full_recv.at[u], device_id=(seq, u), device_id_type=MESH,
        )

    gain = jnp.concatenate([gain_own[j : j + 1] for j in range(pairs)], axis=1)

    def rise(scan, ch):
        up_copy(scan, ch, up_out.at[scan, ch], e_to).wait_recv()
        up_out[scan, ch] = own_in[scan, ch] + gain * up_in[scan, ch]

    def gain_rise(scan):
        gain_copy(scan, gain_own, e_to).wait_recv()
        gain_out[scan] = gain_own[...] * gain_in[scan]

    @pl.when(outer)
    def _():
        gain_copy(early, gain_own, e_to).start()

        def send(ch, _):
            up_copy(early, ch, own_in.at[early, ch], e_to).start()
            return 0

        lax.fori_loop(0, chunks, send, 0)
        gain_rise(late)

        def tell(ch, _):
            gain_far_copy(ch).start()
            return 0

        lax.fori_loop(0, chunks, tell, 0)

        def finish(ch, _):
            rise(late, ch)
            owner_copy(ch).start()
            return 0

        lax.fori_loop(0, chunks, finish, 0)

    lag = min(LAG, chunks)

    @pl.when(~outer)
    def _():
        gain_rise(early)
        gain_copy(early, gain_out.at[early], e_to).start()

        def step(i, _):
            @pl.when(i < chunks)
            def _():
                rise(early, i)
                up_copy(early, i, up_out.at[early, i], e_to).start()

            @pl.when(i == lag)
            def _():
                gain_rise(late)
                gain_copy(late, gain_out.at[late], l_to).start()

            @pl.when(i >= lag)
            def _():
                rise(late, i - lag)
                up_copy(late, i - lag, up_out.at[late, i - lag], l_to).start()

            return 0

        lax.fori_loop(0, chunks + lag, step, 0)

        def hand_out(k, entering):
            from_owner[k] = entering
            back_copy(k).start()
            arrived(gain_at, gain_far_recv, k)
            arrived(at_owner, own_recv, k)
            gains = jnp.concatenate([gain_at[k, j : j + 1] for j in range(pairs)], axis=1)
            return gains * entering + at_owner[k]

        lax.fori_loop(0, groups, hand_out, jnp.zeros((deep, lanes), F32))

    def landed(scan, ch):
        down_copy(scan, ch, e_to).wait_recv()

    def fall(scan, ch, to):
        landed(scan, ch)
        down_out[scan, ch] = own_in[scan, ch] + gain * down_in[scan, ch]
        down_copy(scan, ch, to).start()

    def unit(scan, ch):
        @pl.when(lax.rem(ch + 1, per) == 0)
        def _():
            q = ch // per
            u = scan * parts + q
            state = down_in[scan, pl.ds(q * per, per)].reshape(wide, lanes).astype(BF16)
            part = grads[scan, pl.ds(pl.multiple_of(q * wide, wide), wide)]
            unit_out[u] = part + dot(state, factor[scan], 1, 1)

            @pl.when(u != head)
            def _():
                unit_copy(u).start()

    @pl.when(outer)
    def _():
        def one(i, _):
            fall(early, i, e_to)
            unit(early, i)
            return 0

        lax.fori_loop(0, chunks, one, 0)

        def two(i, _):
            landed(late, i)
            unit(late, i)
            return 0

        lax.fori_loop(0, chunks, two, 0)

    @pl.when(~outer)
    def _():
        def step(i, _):
            @pl.when(i < chunks)
            def _():
                fall(early, i, e_to)

            @pl.when(i >= lag)
            def _():
                fall(late, i - lag, l_to)

            @pl.when(i < chunks)
            def _():
                unit(early, i)

            @pl.when(i >= lag)
            def _():
                unit(late, i - lag)

            return 0

        lax.fori_loop(0, chunks + lag, step, 0)

    spread = lane_head(lanes, heads)
    rising = jnp.zeros((tokens, heads), F32)
    falling = jnp.zeros((tokens, heads), F32)
    start = down_in[0].reshape(STATE, lanes)
    adj = down_in[1].reshape(STATE, lanes)
    for j in range(pairs):
        span = slice(j * PAIR, (j + 1) * PAIR)
        x, g = x_ref[:, span].astype(F32), g_ref[:, span].astype(F32)
        own = spread[span]
        out = within_ref[:, span] + grown_ref[:, span] * dot(c, start[:, span].astype(BF16))
        pushed = left_ref[:, span] * dot(b, adj[:, span].astype(BF16))
        out_ref[:, span] = out.astype(BF16)
        dx_ref[:, span] = (dxw_ref[:, span] + pushed).astype(BF16)
        rising += split_dot(g * out - x * dxw_ref[:, span], own)
        falling += split_dot(x * pushed, own)

    def add(o, total):
        u = lax.rem(head + o, peers)
        unit_from(u).wait_recv()
        return total + unit_in[u]

    full[head] = lax.fori_loop(1, peers, add, unit_out[head])
    for o in range(1, peers):
        full_copy(lax.rem(head + o, peers)).start()

    meet = jnp.sum(start * adj, axis=0, keepdims=True) * gain
    meet = jnp.broadcast_to(meet, (8, lanes))
    high = meet.astype(BF16)
    low = (meet - high.astype(F32)).astype(BF16)
    where = head_of_lane(heads, lanes)
    last = dot(where, high, 1, 1) + dot(where, low, 1, 1)
    dldt_ref[...] = (
        dot(rising, lower(tokens).astype(F32), 0, 0, precision=HIGHEST)
        + dot(falling, lower(tokens, True).astype(F32), 0, 1, precision=HIGHEST)
        + last[:, :1]
    )

    gain_copy(early, gain_own, e_to).wait_send()

    def gone(ch, _):
        up_copy(early, ch, up_out.at[early, ch], e_to).wait_send()
        down_copy(early, ch, e_to).wait_send()

        @pl.when(outer)
        def _():
            owner_copy(ch).wait_send()
            gain_far_copy(ch).wait_send()

        @pl.when(~outer)
        def _():
            up_copy(late, ch, up_out.at[late, ch], l_to).wait_send()
            down_copy(late, ch, l_to).wait_send()
            back_copy(ch).wait_send()

        return 0

    lax.fori_loop(0, chunks, gone, 0)

    @pl.when(~outer)
    def _():
        gain_copy(late, gain_own, l_to).wait_send()

    for o in range(1, peers):
        u = lax.rem(head + o, peers)
        unit_copy(u).wait_send()
        full_copy(u).wait_send()
        full_from(u).wait_recv()
    gc_ref[...] = full[:parts].reshape(STATE, tokens).T
    gb_ref[...] = full[parts:].reshape(STATE, tokens).T


def shards(inputs, log_decay, b_proj, c_proj, grad_out):
    tokens, heads = log_decay.shape
    lanes = heads * HEADDIM
    groups = lax.axis_size("seq") // GROUP
    peers = lax.axis_size("head")
    deep = STATE // groups
    unit = (peers, STATE // (peers // 2), tokens)
    chunk = (2, groups, deep, lanes)
    dma = pltpu.SemaphoreType.DMA
    half = jax.ShapeDtypeStruct(inputs.shape, BF16)
    thin = jax.ShapeDtypeStruct((tokens, STATE), F32)
    whole = pl.BlockSpec(memory_space=VMEM)
    outputs, grad_inputs, grad_decay, grad_b, grad_c = pl.pallas_call(
        main_kernel,
        out_shape=(half, half, jax.ShapeDtypeStruct((heads, tokens), F32), thin, thin),
        in_specs=[whole] * 5,
        out_specs=(whole,) * 5,
        scratch_shapes=[
            pltpu.VMEM((tokens, lanes), F32), pltpu.VMEM((tokens, lanes), F32),
            pltpu.VMEM((tokens, lanes), F32), pltpu.VMEM((tokens, lanes), F32),
            pltpu.VMEM((2, tokens, lanes), BF16), pltpu.VMEM((2, STATE, tokens), F32),
            pltpu.VMEM(chunk, F32), pltpu.VMEM(chunk, F32), pltpu.VMEM(chunk, F32),
            pltpu.VMEM(chunk, F32), pltpu.VMEM(chunk, F32),
            pltpu.VMEM((groups, deep, lanes), F32), pltpu.VMEM((groups, deep, lanes), F32),
            pltpu.VMEM((8, PAIR), F32), pltpu.VMEM((2, 8, PAIR), F32), pltpu.VMEM((2, 8, PAIR), F32),
            pltpu.VMEM((groups, 8, PAIR), F32),
            pltpu.VMEM(unit, F32), pltpu.VMEM(unit, F32), pltpu.VMEM(unit, F32),
            dma((2, groups)), dma((2, groups)), dma((groups,)), dma((groups,)),
            dma((2, groups)), dma((2, groups)), dma((groups,)),
            dma((2,)), dma((2,)), dma((groups,)), dma((groups,)),
            dma((peers,)), dma((peers,)), dma((peers,)), dma((peers,)),
        ],
        compiler_params=pltpu.CompilerParams(
            collective_id=0, has_side_effects=True, vmem_limit_bytes=56 * 2**20
        ),
        name="scan",
    )(inputs, log_decay.T, b_proj, c_proj, grad_out)
    return outputs, grad_inputs, grad_decay.T, grad_b, grad_c


def solution(mesh):
    placed = (P("seq", "head"), P("seq", "head"), P("seq", None), P("seq", None), P("seq", "head"))
    return jax.shard_map(
        shards,
        mesh=mesh,
        in_specs=placed,
        out_specs=(
            P("seq", "head"),
            P("seq", "head"),
            P("seq", "head"),
            P("seq", None),
            P("seq", None),
        ),
        check_vma=False,
    )
```

time: 828 us -> 84.2 us (0.10)
  waiting for transfers between devices: 372 us -> 0 us
  other arithmetic: 140 us -> 0 us
  blocking collectives: 124 us -> 0 us
  matrix products: 86.6 us -> 0 us
  Pallas kernels: 0 us -> 78.7 us
  local copies, waits for them, and re-layouts: 48 us -> 4.72 us
  loops' own time: 37 us -> 0 us
  between operations: 14.6 us -> 0.65 us
    all_gather x2 -> x0, waiting for transfers between devices: 310 us -> none  [entering(): gathered = jax.tree.map(lambda a: lax.all_gather(a, axis), part)]
    unnamed x1 -> x0, blocking collectives: 124 us -> none
    dot_general x87 -> x0, matrix products: 86.6 us -> none  [the longest x30 46.9 us: block_terms(): jnp.einsum('kts,ksp->ktp', weighted, head_signal.astype(jnp.bfloat16), pr...]
    pallas_call x0 -> x1, Pallas kernels: none -> 78.7 us  [shards(): pl.pallas_call(main_kernel, out_shape=(half, half, jax.ShapeDtypeStruct((...]
    add x64 -> x0, other arithmetic: 69.4 us -> none  [the longest x63 68.8 us: combine(): late_gain[:, None, None] * early_state + late_state]
    psum x1 -> x0, waiting for transfers between devices: 62.4 us -> none  [shards(): lax.psum((b_local + b_score, c_local + c_carry + c_score), 'head')]
    another operation x4 -> x0, loops' own time: 37 us -> none  [the longest x2 34.6 us: device_terms(): outs_heads, finals, gains = lax.map(per_head, (head_signal, head_decay))]
    another operation x77 -> x0, other arithmetic: 27.4 us -> none
  transfers between devices with their start and end apart: 3 -> 0, of which waited for: 3 -> 0; matrix products, arithmetic and copies ran while one was open for 1% -> 0% of each run, Pallas kernels for 0% -> 0%
where the time goes in v2:
time: 84.2 us; the launch traced here: 84 us
  Pallas kernels  78.7 us (93%)
  local copies, waits for them, and re-layouts  4.72 us (6%)
    pallas_call x1, Pallas kernels, shards(): pl.pallas_call(main_kernel, out_shape=(half, half, jax.ShapeDtypeStruct((...  78.7 us
    unnamed x13, local copies, waits for them, and re-layouts  4.72 us

profile of v2, /device:TPU:1, one launch (start us, length us, event | category | flops | bytes accessed | tf_op | source)
XLA Modules:
  0.0 84.0 jit_solution(11149884951326615347)
XLA Ops:
  0.6 78.7 %scan.1 = (bf16[256,640]{1,0:T(8,128)(2,1)}, bf16[256,640]{1,0:T(8,128)(2,1)}, f32[10,256]{1,0:T(8,128)}, f32[256,128]{1,0:T(8,128)}, f32[256,128]{1,0:T(8,128)}) custom-call(bf16[256,640]{1,0:T(8,128)(2,1)} %x_ref.1, f32[10,256]{1,0:T(8,128)} %bitcast.2, bf16[256,128]{1,0:T(8,128)(2,1)} %b_ref.1, bf16[256,128]{1,0:T(8,128)(2,1)} %c_ref.1, ...), custom_call_target="tpu_custom_call" | custom-call | tf_op jit(solution)/shard_map/scan/pallas_call | solution.py:448
  79.3 0.0 copy-start
  79.3 1.8 %copy.15 = bf16[256,640]{1,0:T(8,128)(2,1)} copy(bf16[256,640]{1,0:T(8,128)(2,1)} %get-tuple-element.20) | data formatting | bytes 655360
  81.1 0.0 copy-done
  81.1 0.0 copy-start.3
  81.1 0.0 copy-start.2
  81.1 0.7 copy.16
  81.8 0.0 copy-done.3
  81.8 0.6 copy.17
  82.4 0.0 copy-done.2
  82.4 0.0 copy-start.1
  82.4 0.7 copy.18
  83.1 0.3 copy-done.1
  83.4 0.7 copy.19
Async XLA Ops:
  79.3 1.8 %copy-start = (bf16[256,640]{1,0:T(8,128)(2,1)S(1)}, bf16[256,640]{1,0:T(8,128)(2,1)}, u32[]{:S(2)}) copy-start(bf16[256,640]{1,0:T(8,128)(2,1)} %get-tuple-element.21) | copy-start | bytes 983044
  81.1 0.7 copy-start.3
  81.1 1.3 %copy-start.2 = (f32[256,128]{1,0:T(8,128)S(1)}, f32[256,128]{1,0:T(8,128)}, u32[]{:S(2)}) copy-start(f32[256,128]{1,0:T(8,128)} %get-tuple-element.23) | copy-start | bytes 393220
  82.4 1.0 %copy-start.1 = (f32[256,128]{1,0:T(8,128)S(1)}, f32[256,128]{1,0:T(8,128)}, u32[]{:S(2)}) copy-start(f32[256,128]{1,0:T(8,128)} %get-tuple-element.24) | copy-start | bytes 393220

commit v3 on v2

--- a/solution.py
+++ b/solution.py
@@ -57,8 +57,8 @@
 
 
 def main_kernel(
-    x_ref, ldt_ref, b_ref, c_ref, g_ref, out_ref, dx_ref, dldt_ref, gb_ref, gc_ref,
-    grown_ref, left_ref, within_ref, dxw_ref, factor, grads,
+    x_hbm, ldt_hbm, b_hbm, c_hbm, g_hbm, out_ref, dx_ref, dldt_ref, gb_ref, gc_ref,
+    x_ref, ldt_ref, b_ref, c_ref, g_ref, load_sem, grown_ref, left_ref, within_ref, dxw_ref, factor, grads,
     own_in, up_in, up_out, down_in, down_out, at_owner, from_owner,
     gain_own, gain_in, gain_out, gain_at, unit_out, unit_in, full,
     up_send, up_recv, own_recv, own_send, down_recv, down_send, rep_send,
@@ -83,12 +83,28 @@
     ahead = jnp.where(early == 0, 1, -1)
     e_to, l_to = (seq + ahead, head), (seq - ahead, head)
 
+    across = 4 if groups % 16 == 0 else 1
+
     def owner(scan, ch):
-        where = lax.rem(ch + shift, groups)
+        slot = lax.rem(ch + shift, groups)
+        row, turn = lax.rem(slot, across), slot // across
+        where = row * (groups // across) + lax.rem(turn + row, groups // across)
         return (jnp.where(scan == 0, where * GROUP + 1, (groups - 1 - where) * GROUP + 2), head)
 
     scan_owned = jnp.where(place == 1, 0, 1)
-    mine = lax.rem(jnp.where(place == 1, group, groups - 1 - group) + groups - shift, groups)
+    order = jnp.where(place == 1, group, groups - 1 - group)
+    row, turn = order // (groups // across), lax.rem(order, groups // across)
+    turn = lax.rem(turn - row + groups, groups // across)
+    mine = lax.rem(turn * across + row + groups - shift, groups)
+
+    loads = [
+        pltpu.make_async_copy(source, target, load_sem.at[i])
+        for i, (source, target) in enumerate(
+            ((ldt_hbm, ldt_ref), (x_hbm, x_ref), (b_hbm, b_ref), (g_hbm, g_ref), (c_hbm, c_ref))
+        )
+    ]
+    for load in loads:
+        load.start()
 
     barrier = pltpu.get_barrier_semaphore()
 
@@ -117,6 +133,8 @@
     for step in range(1, peers):
         greet((seq, lax.rem(head + step, peers)))
 
+    for load in loads:
+        load.wait()
     ldt = ldt_ref[...]
     prefix, grown, left = decays(ldt)
     grown_ref[...] = grown
@@ -433,6 +451,15 @@
     gb_ref[...] = full[parts:].reshape(STATE, tokens).T
 
 
+def store_kernel(*refs):
+    sems = refs[-1]
+    copies = [pltpu.make_async_copy(refs[i], refs[5 + i], sems.at[i]) for i in range(5)]
+    for copy in copies:
+        copy.start()
+    for copy in copies:
+        copy.wait()
+
+
 def shards(inputs, log_decay, b_proj, c_proj, grad_out):
     tokens, heads = log_decay.shape
     lanes = heads * HEADDIM
@@ -445,12 +472,16 @@
     half = jax.ShapeDtypeStruct(inputs.shape, BF16)
     thin = jax.ShapeDtypeStruct((tokens, STATE), F32)
     whole = pl.BlockSpec(memory_space=VMEM)
-    outputs, grad_inputs, grad_decay, grad_b, grad_c = pl.pallas_call(
+    results = (half, half, jax.ShapeDtypeStruct((heads, tokens), F32), thin, thin)
+    held = pl.pallas_call(
         main_kernel,
-        out_shape=(half, half, jax.ShapeDtypeStruct((heads, tokens), F32), thin, thin),
-        in_specs=[whole] * 5,
+        out_shape=tuple(pltpu.VMEM(a.shape, a.dtype) for a in results),
+        in_specs=[pl.BlockSpec(memory_space=pl.ANY)] * 5,
         out_specs=(whole,) * 5,
         scratch_shapes=[
+            pltpu.VMEM((tokens, lanes), BF16), pltpu.VMEM((heads, tokens), F32),
+            pltpu.VMEM((tokens, STATE), BF16), pltpu.VMEM((tokens, STATE), BF16),
+            pltpu.VMEM((tokens, lanes), BF16), dma((5,)),
             pltpu.VMEM((tokens, lanes), F32), pltpu.VMEM((tokens, lanes), F32),
             pltpu.VMEM((tokens, lanes), F32), pltpu.VMEM((tokens, lanes), F32),
             pltpu.VMEM((2, tokens, lanes), BF16), pltpu.VMEM((2, STATE, tokens), F32),
@@ -470,6 +501,14 @@
         ),
         name="scan",
     )(inputs, log_decay.T, b_proj, c_proj, grad_out)
+    outputs, grad_inputs, grad_decay, grad_b, grad_c = pl.pallas_call(
+        store_kernel,
+        out_shape=results,
+        in_specs=[pl.BlockSpec(memory_space=pl.ANY)] * 5,
+        out_specs=(pl.BlockSpec(memory_space=pl.ANY),) * 5,
+        scratch_shapes=[dma((5,))],
+        name="store",
+    )(*(pltpu.with_memory_space_constraint(array, VMEM) for array in held))
     return outputs, grad_inputs, grad_decay.T, grad_b, grad_c
 
 

time: 84.2 us -> 77.7 us (0.923)
  local copies, waits for them, and re-layouts: 4.72 us -> 0 us
  Pallas kernels: 78.7 us -> 76.9 us
    unnamed x13 -> x0, local copies, waits for them, and re-layouts: 4.72 us -> none
    pallas_call x1 -> x2, Pallas kernels: 78.7 us -> 76.9 us  [the longest x1 75.9 us: shards(): pl.pallas_call(main_kernel, out_shape=tuple((pltpu.VMEM(a.shape, a.dtype)...]
where the time goes in v3:
time: 77.7 us; the launch traced here: 77.5 us
  Pallas kernels  76.9 us (99%)
    pallas_call x1, Pallas kernels, shards(): pl.pallas_call(main_kernel, out_shape=tuple((pltpu.VMEM(a.shape, a.dtype)...  75.9 us

profile of v3, /device:TPU:1, one launch (start us, length us, event | category | flops | bytes accessed | tf_op | source)
XLA Modules:
  0.0 77.5 jit_solution(17525595164062186469)
XLA Ops:
  0.6 75.9 %scan.1 = (bf16[256,640]{1,0:T(8,128)(2,1)S(1)}, bf16[256,640]{1,0:T(8,128)(2,1)S(1)}, f32[10,256]{1,0:T(8,128)S(1)}, f32[256,128]{1,0:T(8,128)S(1)}, f32[256,128]{1,0:T(8,128)S(1)}) custom-call(bf16[256,640]{1,0:T(8,128)(2,1)} %x_hbm.1, f32[10,256]{1,0:T(8,128)} %bitcast.2, bf16[256,128]{1,0:T(8,128)(2,1)} %b_hbm.1, bf16[256,128]{1,0:T(8,128)(2,1)} %c_hbm.1, ...), custom_call_target="tpu_custom_call" | custom-call | tf_op jit(solution)/shard_map/scan/pallas_call | solution.py:476
  76.5 1.0 %store.1 = (bf16[256,640]{1,0:T(8,128)(2,1)}, bf16[256,640]{1,0:T(8,128)(2,1)}, f32[10,256]{1,0:T(8,128)}, f32[256,128]{1,0:T(8,128)}, f32[256,128]{1,0:T(8,128)}) custom-call(bf16[256,640]{1,0:T(8,128)(2,1)S(1)} %get-tuple-element.15.refs_0_, bf16[256,640]{1,0:T(8,128)(2,1)S(1)} %get-tuple-element.16.refs_1_, f32[10,256]{1,0:T(8,128)S(1)} %get-tuple-element.17.refs_2_, ...), custom_call_target="tpu_custom_call" | custom-call | tf_op jit(solution)/shard_map/store/pallas_call | solution.py:504

commit v4 on v3

--- a/solution.py
+++ b/solution.py
@@ -9,7 +9,7 @@
 STATE = 128
 PAIR = 128
 GROUP = 4
-LAG = 5
+LAG = 6
 MESH = pl.DeviceIdType.MESH
 F32 = jnp.float32
 BF16 = jnp.bfloat16
@@ -60,9 +60,9 @@
     x_hbm, ldt_hbm, b_hbm, c_hbm, g_hbm, out_ref, dx_ref, dldt_ref, gb_ref, gc_ref,
     x_ref, ldt_ref, b_ref, c_ref, g_ref, load_sem, grown_ref, left_ref, within_ref, dxw_ref, factor, grads,
     own_in, up_in, up_out, down_in, down_out, at_owner, from_owner,
-    gain_own, gain_in, gain_out, gain_at, unit_out, unit_in, full,
+    gain_own, gain_in, gain_out, gain_at, gain_wide, unit_out, unit_in, full, last_in,
     up_send, up_recv, own_recv, own_send, down_recv, down_send, rep_send,
-    gain_send, gain_recv, gain_far_send, gain_far_recv, unit_send, unit_recv, full_send, full_recv,
+    gain_send, gain_recv, gain_far_send, gain_far_recv, unit_send, unit_recv, full_send, full_recv, last_send, last_recv,
 ):
     heads, tokens = ldt_ref.shape
     lanes = heads * HEADDIM
@@ -147,30 +147,38 @@
     factor[1] = scaled
     own_in[0] = dot(b, scaled, 0, 0).reshape(chunks, deep, lanes)
     own_in[1] = dot(c, risen, 0, 0).reshape(chunks, deep, lanes)
-    for j in range(pairs):
-        gain_own[j : j + 1] = grown[tokens - 1 : tokens, j * PAIR : (j + 1) * PAIR]
-    gain_own[pairs:] = jnp.zeros((8 - pairs, PAIR), F32)
-
-    scores = dot(c, b, 1, 1)
-    causal = lower(tokens)
-    first = lax.broadcasted_iota(jnp.int32, (tokens, PAIR), 1) < HEADDIM
-    total = jnp.zeros((tokens, tokens), F32)
-    for j in range(pairs):
-        span = slice(j * PAIR, (j + 1) * PAIR)
-        xp, gp = x_ref[:, span], g_ref[:, span]
-        found = []
-        for e in range(2):
-            h = 2 * j + e
-            decay = jnp.where(causal, jnp.exp(prefix[:, h : h + 1] - rows[h : h + 1]), 0.0)
-            weighted = (scores * decay).astype(BF16)
-            own = jnp.where(first if e == 0 else ~first, gp.astype(F32), 0.0).astype(BF16)
-            total += dot(own, xp, 1, 1) * decay
-            found.append((dot(weighted, xp), dot(weighted, gp, 0, 0)))
-        within_ref[:, span] = jnp.where(first, found[0][0], found[1][0])
-        dxw_ref[:, span] = jnp.where(first, found[0][1], found[1][1])
-    halved = total.astype(BF16)
-    grads[0] = dot(b, halved, 0, 1)
-    grads[1] = dot(c, halved, 0, 0)
+    gain = grown[tokens - 1 : tokens]
+    gain_own[...] = jnp.concatenate(
+        [jnp.exp(prefix[tokens - 1 : tokens]), jnp.zeros((1, PAIR - heads), F32)], axis=1
+    )
+
+    def attend():
+        scores = dot(c, b, 1, 1)
+        causal = lower(tokens)
+        first = lax.broadcasted_iota(jnp.int32, (tokens, PAIR), 1) < HEADDIM
+        total = jnp.zeros((tokens, tokens), F32)
+        for j in range(pairs):
+            span = slice(j * PAIR, (j + 1) * PAIR)
+            xp, gp = x_ref[:, span], g_ref[:, span]
+            found = []
+            for e in range(2):
+                h = 2 * j + e
+                decay = jnp.where(causal, jnp.exp(prefix[:, h : h + 1] - rows[h : h + 1]), 0.0)
+                weighted = (scores * decay).astype(BF16)
+                own = jnp.where(first if e == 0 else ~first, gp.astype(F32), 0.0).astype(BF16)
+                total += dot(own, xp, 1, 1) * decay
+                found.append((dot(weighted, xp), dot(weighted, gp, 0, 0)))
+            within_ref[:, span] = jnp.where(first, found[0][0], found[1][0])
+            dxw_ref[:, span] = jnp.where(first, found[0][1], found[1][1])
+        halved = total.astype(BF16)
+        grads[0] = dot(b, halved, 0, 1)
+        grads[1] = dot(c, halved, 0, 0)
+
+    second = lax.rem(head, 2) == 1
+
+    @pl.when(~second)
+    def _():
+        attend()
 
     @pl.when(outer)
     def _():
@@ -179,6 +187,10 @@
     @pl.when(~outer)
     def _():
         pl.semaphore_wait(barrier, 2 * groups + 1 + peers - 1)
+
+    @pl.when(second)
+    def _():
+        attend()
 
     def up_copy(scan, ch, source, to):
         return pltpu.make_async_remote_copy(
@@ -237,6 +249,20 @@
             recv_sem=unit_recv.at[u], device_id=(seq, u), device_id_type=MESH,
         )
 
+    final = late * parts + parts - 1
+
+    def last_copy(u):
+        return pltpu.make_async_remote_copy(
+            src_ref=unit_out.at[final], dst_ref=last_in.at[head], send_sem=last_send.at[u],
+            recv_sem=last_recv.at[head], device_id=(seq, u), device_id_type=MESH,
+        )
+
+    def last_from(u):
+        return pltpu.make_async_remote_copy(
+            src_ref=last_in.at[u], dst_ref=last_in.at[u], send_sem=last_send.at[u],
+            recv_sem=last_recv.at[u], device_id=(seq, u), device_id_type=MESH,
+        )
+
     def full_copy(u):
         return pltpu.make_async_remote_copy(
             src_ref=full.at[head], dst_ref=full.at[head], send_sem=full_send.at[u],
@@ -248,8 +274,6 @@
             src_ref=full.at[u], dst_ref=full.at[u], send_sem=full_send.at[u],
             recv_sem=full_recv.at[u], device_id=(seq, u), device_id_type=MESH,
         )
-
-    gain = jnp.concatenate([gain_own[j : j + 1] for j in range(pairs)], axis=1)
 
     def rise(scan, ch):
         up_copy(scan, ch, up_out.at[scan, ch], e_to).wait_recv()
@@ -271,14 +295,21 @@
         gain_rise(late)
 
         def tell(ch, _):
-            gain_far_copy(ch).start()
+            @pl.when(rank < groups - 1)
+            def _():
+                gain_far_copy(ch).start()
+
             return 0
 
         lax.fori_loop(0, chunks, tell, 0)
 
         def finish(ch, _):
             rise(late, ch)
-            owner_copy(ch).start()
+
+            @pl.when(rank < groups - 1)
+            def _():
+                owner_copy(ch).start()
+
             return 0
 
         lax.fori_loop(0, chunks, finish, 0)
@@ -309,22 +340,38 @@
             return 0
 
         lax.fori_loop(0, chunks + lag, step, 0)
+
+        def told(k, _):
+            arrived(gain_at, gain_far_recv, k)
+            return 0
+
+        lax.fori_loop(0, groups - 1, told, 0)
+        gain_at[groups - 1] = jnp.zeros((1, PAIR), F32)
+        gains = jnp.concatenate([gain_at[k] for k in range(groups)], axis=0)
+        r = lax.broadcasted_iota(jnp.int32, (PAIR, lanes), 0)
+        l = lax.broadcasted_iota(jnp.int32, (PAIR, lanes), 1)
+        gain_wide[...] = split_dot(gains, jnp.where(l // HEADDIM == r, 1.0, 0.0).astype(BF16))
+        arrived(at_owner, own_recv, 0)
 
         def hand_out(k, entering):
             from_owner[k] = entering
             back_copy(k).start()
-            arrived(gain_at, gain_far_recv, k)
-            arrived(at_owner, own_recv, k)
-            gains = jnp.concatenate([gain_at[k, j : j + 1] for j in range(pairs)], axis=1)
-            return gains * entering + at_owner[k]
-
-        lax.fori_loop(0, groups, hand_out, jnp.zeros((deep, lanes), F32))
+
+            @pl.when(k < groups - 1)
+            def _():
+                arrived(at_owner, own_recv, k)
+
+            return gain_wide[pl.ds(k, 1)] * entering + at_owner[k]
+
+        at_owner[groups - 1] = jnp.zeros((deep, lanes), F32)
+        lax.fori_loop(1, groups, hand_out, at_owner[0])
 
     def landed(scan, ch):
         down_copy(scan, ch, e_to).wait_recv()
 
+    begins = jnp.where(early == 0, group, groups - 1 - group) == 0
+
     def fall(scan, ch, to):
-        landed(scan, ch)
         down_out[scan, ch] = own_in[scan, ch] + gain * down_in[scan, ch]
         down_copy(scan, ch, to).start()
 
@@ -337,13 +384,26 @@
             part = grads[scan, pl.ds(pl.multiple_of(q * wide, wide), wide)]
             unit_out[u] = part + dot(state, factor[scan], 1, 1)
 
-            @pl.when(u != head)
+            @pl.when((u != head) & (u != final))
             def _():
                 unit_copy(u).start()
 
+            @pl.when(u == final)
+            def _():
+                for o in range(1, peers):
+                    last_copy(lax.rem(head + o, peers)).start()
+
     @pl.when(outer)
     def _():
         def one(i, _):
+            @pl.when(begins)
+            def _():
+                down_in[early, i] = jnp.zeros((deep, lanes), F32)
+
+            @pl.when(~begins)
+            def _():
+                landed(early, i)
+
             fall(early, i, e_to)
             unit(early, i)
             return 0
@@ -362,10 +422,12 @@
         def step(i, _):
             @pl.when(i < chunks)
             def _():
+                landed(early, i)
                 fall(early, i, e_to)
 
             @pl.when(i >= lag)
             def _():
+                landed(late, i - lag)
                 fall(late, i - lag, l_to)
 
             @pl.when(i < chunks)
@@ -385,6 +447,17 @@
     falling = jnp.zeros((tokens, heads), F32)
     start = down_in[0].reshape(STATE, lanes)
     adj = down_in[1].reshape(STATE, lanes)
+    @pl.when(head != final)
+    def _():
+        def add(o, total):
+            u = lax.rem(head + o, peers)
+            unit_from(u).wait_recv()
+            return total + unit_in[u]
+
+        full[head] = lax.fori_loop(1, peers, add, unit_out[head])
+        for o in range(1, peers):
+            full_copy(lax.rem(head + o, peers)).start()
+
     for j in range(pairs):
         span = slice(j * PAIR, (j + 1) * PAIR)
         x, g = x_ref[:, span].astype(F32), g_ref[:, span].astype(F32)
@@ -395,15 +468,6 @@
         dx_ref[:, span] = (dxw_ref[:, span] + pushed).astype(BF16)
         rising += split_dot(g * out - x * dxw_ref[:, span], own)
         falling += split_dot(x * pushed, own)
-
-    def add(o, total):
-        u = lax.rem(head + o, peers)
-        unit_from(u).wait_recv()
-        return total + unit_in[u]
-
-    full[head] = lax.fori_loop(1, peers, add, unit_out[head])
-    for o in range(1, peers):
-        full_copy(lax.rem(head + o, peers)).start()
 
     meet = jnp.sum(start * adj, axis=0, keepdims=True) * gain
     meet = jnp.broadcast_to(meet, (8, lanes))
@@ -425,14 +489,19 @@
 
         @pl.when(outer)
         def _():
-            owner_copy(ch).wait_send()
-            gain_far_copy(ch).wait_send()
+            @pl.when(rank < groups - 1)
+            def _():
+                owner_copy(ch).wait_send()
+                gain_far_copy(ch).wait_send()
 
         @pl.when(~outer)
         def _():
             up_copy(late, ch, up_out.at[late, ch], l_to).wait_send()
             down_copy(late, ch, l_to).wait_send()
-            back_copy(ch).wait_send()
+
+            @pl.when(ch > 0)
+            def _():
+                back_copy(ch).wait_send()
 
         return 0
 
@@ -442,11 +511,25 @@
     def _():
         gain_copy(late, gain_own, l_to).wait_send()
 
+    last_in[head] = unit_out[final]
     for o in range(1, peers):
         u = lax.rem(head + o, peers)
-        unit_copy(u).wait_send()
-        full_copy(u).wait_send()
-        full_from(u).wait_recv()
+        last_copy(u).wait_send()
+        last_from(u).wait_recv()
+
+        @pl.when(u != final)
+        def _():
+            unit_copy(u).wait_send()
+            full_from(u).wait_recv()
+
+        @pl.when(head != final)
+        def _():
+            full_copy(u).wait_send()
+
+    total = last_in[0]
+    for u in range(1, peers):
+        total += last_in[u]
+    full[final] = total
     gc_ref[...] = full[:parts].reshape(STATE, tokens).T
     gb_ref[...] = full[parts:].reshape(STATE, tokens).T
 
@@ -488,13 +571,13 @@
             pltpu.VMEM(chunk, F32), pltpu.VMEM(chunk, F32), pltpu.VMEM(chunk, F32),
             pltpu.VMEM(chunk, F32), pltpu.VMEM(chunk, F32),
             pltpu.VMEM((groups, deep, lanes), F32), pltpu.VMEM((groups, deep, lanes), F32),
-            pltpu.VMEM((8, PAIR), F32), pltpu.VMEM((2, 8, PAIR), F32), pltpu.VMEM((2, 8, PAIR), F32),
-            pltpu.VMEM((groups, 8, PAIR), F32),
-            pltpu.VMEM(unit, F32), pltpu.VMEM(unit, F32), pltpu.VMEM(unit, F32),
+            pltpu.VMEM((1, PAIR), F32), pltpu.VMEM((2, 1, PAIR), F32), pltpu.VMEM((2, 1, PAIR), F32),
+            pltpu.VMEM((groups, 1, PAIR), F32), pltpu.VMEM((groups, lanes), F32),
+            pltpu.VMEM(unit, F32), pltpu.VMEM(unit, F32), pltpu.VMEM(unit, F32), pltpu.VMEM(unit, F32),
             dma((2, groups)), dma((2, groups)), dma((groups,)), dma((groups,)),
             dma((2, groups)), dma((2, groups)), dma((groups,)),
             dma((2,)), dma((2,)), dma((groups,)), dma((groups,)),
-            dma((peers,)), dma((peers,)), dma((peers,)), dma((peers,)),
+            dma((peers,)), dma((peers,)), dma((peers,)), dma((peers,)), dma((peers,)), dma((peers,)),
         ],
         compiler_params=pltpu.CompilerParams(
             collective_id=0, has_side_effects=True, vmem_limit_bytes=56 * 2**20

time: 77.7 us -> 72.9 us (0.938)
  Pallas kernels: 76.9 us -> 72.1 us
    pallas_call x1, Pallas kernels: 75.9 us -> 71.1 us  [shards(): pl.pallas_call(main_kernel, out_shape=tuple((pltpu.VMEM(a.shape, a.dtype)...]
where the time goes in v4:
time: 72.9 us; the launch traced here: 72.7 us
  Pallas kernels  72.1 us (99%)
    pallas_call x1, Pallas kernels, shards(): pl.pallas_call(main_kernel, out_shape=tuple((pltpu.VMEM(a.shape, a.dtype)...  71.1 us

profile of v4, /device:TPU:1, one launch (start us, length us, event | category | flops | bytes accessed | tf_op | source)
XLA Modules:
  0.0 72.7 jit_solution(16114624426580941756)
XLA Ops:
  0.6 71.1 %scan.1 = (bf16[256,640]{1,0:T(8,128)(2,1)S(1)}, bf16[256,640]{1,0:T(8,128)(2,1)S(1)}, f32[10,256]{1,0:T(8,128)S(1)}, f32[256,128]{1,0:T(8,128)S(1)}, f32[256,128]{1,0:T(8,128)S(1)}) custom-call(bf16[256,640]{1,0:T(8,128)(2,1)} %x_hbm.1, f32[10,256]{1,0:T(8,128)} %bitcast.2, bf16[256,128]{1,0:T(8,128)(2,1)} %b_hbm.1, bf16[256,128]{1,0:T(8,128)(2,1)} %c_hbm.1, ...), custom_call_target="tpu_custom_call" | custom-call | tf_op jit(solution)/shard_map/scan/pallas_call | solution.py:559
  71.7 1.0 %store.1 = (bf16[256,640]{1,0:T(8,128)(2,1)}, bf16[256,640]{1,0:T(8,128)(2,1)}, f32[10,256]{1,0:T(8,128)}, f32[256,128]{1,0:T(8,128)}, f32[256,128]{1,0:T(8,128)}) custom-call(bf16[256,640]{1,0:T(8,128)(2,1)S(1)} %get-tuple-element.15.refs_0_, bf16[256,640]{1,0:T(8,128)(2,1)S(1)} %get-tuple-element.16.refs_1_, f32[10,256]{1,0:T(8,128)S(1)} %get-tuple-element.17.refs_2_, ...), custom_call_target="tpu_custom_call" | custom-call | tf_op jit(solution)/shard_map/store/pallas_call | solution.py:587

commit v5 on v4

--- a/solution.py
+++ b/solution.py
@@ -314,7 +314,7 @@
 
         lax.fori_loop(0, chunks, finish, 0)
 
-    lag = min(LAG, chunks)
+    lag = jnp.where(second, min(5, chunks), min(7, chunks))
 
     @pl.when(~outer)
     def _():
@@ -405,10 +405,15 @@
                 landed(early, i)
 
             fall(early, i, e_to)
+            return 0
+
+        lax.fori_loop(0, chunks, one, 0)
+
+        def add(i, _):
             unit(early, i)
             return 0
 
-        lax.fori_loop(0, chunks, one, 0)
+        lax.fori_loop(0, chunks, add, 0)
 
         def two(i, _):
             landed(late, i)

time: 72.9 us -> 72.4 us (level)
  no operation moved by 1% of the time
where the time goes in v5:
time: 72.4 us; the launch traced here: 72.2 us
  Pallas kernels  71.6 us (99%)
    pallas_call x1, Pallas kernels, shards(): pl.pallas_call(main_kernel, out_shape=tuple((pltpu.VMEM(a.shape, a.dtype)...  70.6 us

profile of v5, /device:TPU:1, one launch (start us, length us, event | category | flops | bytes accessed | tf_op | source)
XLA Modules:
  0.0 72.2 jit_solution(6861199760092844657)
XLA Ops:
  0.6 70.6 %scan.1 = (bf16[256,640]{1,0:T(8,128)(2,1)S(1)}, bf16[256,640]{1,0:T(8,128)(2,1)S(1)}, f32[10,256]{1,0:T(8,128)S(1)}, f32[256,128]{1,0:T(8,128)S(1)}, f32[256,128]{1,0:T(8,128)S(1)}) custom-call(bf16[256,640]{1,0:T(8,128)(2,1)} %x_hbm.1, f32[10,256]{1,0:T(8,128)} %bitcast.2, bf16[256,128]{1,0:T(8,128)(2,1)} %b_hbm.1, bf16[256,128]{1,0:T(8,128)(2,1)} %c_hbm.1, ...), custom_call_target="tpu_custom_call" | custom-call | tf_op jit(solution)/shard_map/scan/pallas_call | solution.py:564
  71.3 1.0 %store.1 = (bf16[256,640]{1,0:T(8,128)(2,1)}, bf16[256,640]{1,0:T(8,128)(2,1)}, f32[10,256]{1,0:T(8,128)}, f32[256,128]{1,0:T(8,128)}, f32[256,128]{1,0:T(8,128)}) custom-call(bf16[256,640]{1,0:T(8,128)(2,1)S(1)} %get-tuple-element.15.refs_0_, bf16[256,640]{1,0:T(8,128)(2,1)S(1)} %get-tuple-element.16.refs_1_, f32[10,256]{1,0:T(8,128)S(1)} %get-tuple-element.17.refs_2_, ...), custom_call_target="tpu_custom_call" | custom-call | tf_op jit(solution)/shard_map/store/pallas_call | solution.py:592
